TPU v7x, 512 devices: a whole 4x4x16 slice. The times are simulated.
512 devices in a mesh: seq: 64 (over y_hi, z, core), head: 8 (over x, y_lo).
Axes of the slice: x: 4, y: 4 (y_hi: 2, y_lo: 2; y = y_hi * 2 + y_lo), z: 16, core: 2. Of those that a mesh axis runs over, the one named last changes fastest.
Arguments:
- latent: bfloat16 [8192, 576], P('seq'), may hold values from -7 to 7
- queries: bfloat16 [8192, 8, 576], P('seq', 'head'), may hold values from -66 to 66
- grad_out: bfloat16 [8192, 8, 512], P('seq', 'head'), may hold values from -6 to 6
- doc_lengths: int32 [8], replicated, may hold values from 1 to 5120, 8192 in all
Outputs:
- grad_queries: bfloat16 [8192, 8, 576], P('seq', 'head')
- grad_latent: bfloat16 [8192, 576], P(('seq', 'head'))
Inputs may be any that keep to these rules, and one draw needn't show every extreme that they name: `doc_lengths`: the lengths sum to 8192; the longest is exactly 5120.
All inputs are finite; a program needn't handle non-finite values.
Results may differ from a plain program's by a relative error of at most 0.0085.
Values may be sent and summed in bfloat16 or wider, within the bound.
A program may use at most 64 MiB of HBM per device.

v0:
```python
import jax
import jax.numpy as jnp
from jax import lax
from jax.sharding import PartitionSpec as P

softmax_scale = 0.07216878364870322
far_below = -1e30


def merged(value, axis, join):
    pieces = jax.tree.map(lambda part: lax.all_gather(part, axis), value)
    head = jax.tree.map(lambda part: part[0], pieces)
    tail = jax.tree.map(lambda part: part[1:], pieces)
    subtotal, _ = lax.scan(lambda subtotal, section: (join(subtotal, section), None), head, tail)
    return subtotal


def document_firsts(doc_lengths, positions):
    doc_ends = jnp.cumsum(doc_lengths)
    doc_firsts = doc_ends - doc_lengths
    inside = doc_firsts[None, :] <= positions[:, None]
    return jnp.max(jnp.where(inside, doc_firsts[None, :], 0), axis=1)


def merge_pair(first, second):
    larger = jnp.maximum(first[0], second[0])
    first_scale = jnp.exp(first[0] - larger)
    second_scale = jnp.exp(second[0] - larger)
    return (larger, first[1] * first_scale + second[1] * second_scale)


def local(latent, queries, grad_out, doc_lengths):
    row_count = queries.shape[0]
    width = latent.shape[1]
    value_width = grad_out.shape[2]
    head_count = lax.axis_size("head")
    seq_count = lax.axis_size("seq")
    sub_rows = row_count // head_count
    seq_place = lax.axis_index("seq")
    head_place = lax.axis_index("head")
    all_queries, all_grads = (
        lax.all_gather(queries, "head", axis=1, tiled=True),
        lax.all_gather(grad_out, "head", axis=1, tiled=True),
    )
    all_keys = lax.all_gather(latent, "seq", axis=0, tiled=True)
    grouped = all_keys.reshape(seq_count, head_count, sub_rows, width)
    key_rows = lax.dynamic_index_in_dim(grouped, head_place, 1, keepdims=False).reshape(
        seq_count * sub_rows, width
    )
    key_places = (
        jnp.arange(seq_count, dtype=jnp.int32)[:, None] * row_count
        + head_place * sub_rows
        + jnp.arange(sub_rows, dtype=jnp.int32)[None, :]
    ).reshape(-1)
    query_places = seq_place * row_count + jnp.arange(row_count, dtype=jnp.int32)
    doc_first = document_firsts(doc_lengths, query_places)
    allowed = (key_places[None, :] >= doc_first[:, None]) & (
        key_places[None, :] <= query_places[:, None]
    )
    allowed = allowed[:, None, :]
    scores = (
        jnp.einsum("qhd,kd->qhk", all_queries, key_rows, preferred_element_type=jnp.float32)
        * softmax_scale
    )
    local_max = jnp.max(jnp.where(allowed, scores, far_below), axis=2)
    shifted = jnp.where(allowed, jnp.exp(scores - local_max[..., None]), 0.0)
    local_total = jnp.sum(shifted, axis=2)
    value_rows = key_rows[:, :value_width]
    prob_grad = jnp.einsum("qhv,kv->qhk", all_grads, value_rows, preferred_element_type=jnp.float32)
    row_max, row_total = merged((local_max, local_total), "head", merge_pair)
    probabilities = shifted * (jnp.exp(local_max - row_max) / row_total)[..., None]
    centred = lax.psum(jnp.sum(probabilities * prob_grad, axis=2), "head")
    score_grad = (probabilities * (prob_grad - centred[..., None]) * softmax_scale).astype(
        jnp.bfloat16
    )
    prob_half = probabilities.astype(jnp.bfloat16)
    latent_part = jnp.einsum(
        "qhk,qhd->kd", score_grad, all_queries, preferred_element_type=jnp.float32
    )
    value_part = jnp.einsum("qhk,qhv->kv", prob_half, all_grads, preferred_element_type=jnp.float32)
    latent_part = latent_part + jnp.pad(value_part, ((0, 0), (0, width - value_width)))
    grad_latent = lax.psum_scatter(latent_part, "seq", scatter_dimension=0, tiled=True).astype(
        jnp.bfloat16
    )
    head_grads = lax.all_to_all(score_grad, "head", split_axis=1, concat_axis=2, tiled=True)
    arranged = head_grads.reshape(row_count, queries.shape[1], head_count, seq_count, sub_rows)
    grad_queries = jnp.einsum(
        "qhgsr,sgrd->qhd", arranged, grouped, preferred_element_type=jnp.float32
    ).astype(jnp.bfloat16)
    return (grad_queries, grad_latent)


def solution(mesh):
    placed = (P("seq", None), P("seq", "head", None), P("seq", "head", None), P())
    return jax.shard_map(
        local,
        mesh=mesh,
        in_specs=placed,
        out_specs=(P("seq", "head", None), P(("seq", "head"), None)),
        check_vma=False,
    )
```

profile of v0, /device:TPU:1, one launch (start us, length us, event | category | flops | bytes accessed | tf_op | source)
XLA Modules:
  0.0 541.2 jit_solution(2795224061735399715)
XLA Ops:
  7.2 1.7 copy.25
  9.0 0.7 all-gather.8.cloned.1.call-update
  9.7 0.7 all-gather.10.cloned.1.call-update
  10.5 0.8 reduce-window.9
  11.3 0.7 bitcast_subtract_fusion.3
  12.1 0.1 select_reduce_fusion
  12.2 0.2 compare_and_fusion
  12.4 177.3 %all-gather.6.cloned.1.call-done = bf16[8192,576]{1,0:T(8,128)(2,1)} async-done(((bf16[128,576]{1,0:T(8,128)(2,1)}), bf16[8192,576]{1,0:T(8,128)(2,1)}) %all-gather.6.cloned.1.call-update) | async-done | bytes 9437200 | tf_op jit(solution)/shard_map/all_gather | solution.py:45
  189.8 1.4 constant_dynamic-slice_fusion
  191.2 38.6 %all-gather.8.cloned.1.call-done = bf16[128,8,576]{0,2,1:T(8,128)(2,1)} async-done(((bf16[128,1,576]{0,2,1:T(8,128)(2,1)}), bf16[128,8,576]{0,2,1:T(8,128)(2,1)}) %all-gather.8.cloned.1.call-update) | async-done | bytes 1179664 | tf_op jit(solution)/shard_map/all_gather | solution.py:42
  229.9 3.1 fusion.8
  233.0 21.7 %all-gather = f32[1024,8]{0,1:T(8,128)S(1)} all-gather(f32[128,8]{0,1:T(8,128)S(1)} %get-tuple-element.44), channel_id=2, replica_groups=mesh['seq'=64,'head'=8] {'head'}, dimensions={0}, use_global_device_ids=true | all-gather | bytes 36864 | tf_op jit(solution)/shard_map/all_gather | solution.py:11
  254.7 0.9 fusion.25
  255.6 22.7 %all-gather.1 = f32[1024,8]{0,1:T(8,128)S(1)} all-gather(f32[128,8]{0,1:T(8,128)S(1)} %fusion.25), channel_id=3, replica_groups=mesh['seq'=64,'head'=8] {'head'}, dimensions={0}, use_global_device_ids=true | all-gather | bytes 36864 | tf_op jit(solution)/shard_map/all_gather | solution.py:11
  278.3 0.2 while.12
  278.6 6.1 %fusion.4 = (f32[128,8]{0,1:T(8,128)S(1)}, f32[1024,128,8]{1,0,2:T(8,128)}) fusion(f32[128,8]{0,1:T(8,128)S(1)} %exponential_divide_fusion, f32[128,8]{0,1:T(8,128)S(1)} %get-tuple-element.44, f32[1024,128,8]{1,0,2:T(8,128)} %copy-done, pred[128,1024]{0,1:T(8,128)(4,1)S(1)} %compare_and_fusion, bf16[128,8,512]{2,0,1:T(8,128)(2,1)} %all-gather.10.cloned.1.call-done, ...), kind=kOutput, calls=%fused_computation.9 | convolution fusion | flops 1080032256 | bytes 10629120 | tf_op jit(solution)/shard_map/qhv,kv->qhk/dot_general | solution.py:69
  284.8 14.3 %psum.7 = f32[128,8]{0,1:T(8,128)S(1)} all-reduce(f32[128,8]{0,1:T(8,128)S(1)} %get-tuple-element.46), channel_id=1, replica_groups=mesh['seq'=64,'head'=8] {'head'}, use_global_device_ids=true, to_apply=%region_7.8 | all-reduce | flops 1024 | bytes 8192 | tf_op jit(solution)/shard_map/psum | solution.py:72
  299.1 5.0 fusion.7
  304.2 1.3 fusion.13
  305.5 3.4 bitcast_add_fusion
  308.9 18.1 %all_to_all.4 = bf16[128,8,1024]{0,2,1:T(8,128)(2,1)S(1)} all-to-all(bf16[128,8,1024]{0,2,1:T(8,128)(2,1)S(1)} %fusion.7), channel_id=1, replica_groups=mesh['seq'=64,'head'=8] {'head'}, dimensions={1} | all-to-all | bytes 4194304 | tf_op jit(solution)/shard_map/all_to_all | solution.py:85
  327.0 8.7 %fusion.20 = bf16[128,1,576]{0,2,1:T(8,128)(2,1)} fusion(bf16[128,8,64,16]{0,3,2,1:T(8,128)(2,1)S(1)} %bitcast.81, bf16[64,8,16,576]{3,2,1,0:T(8,128)(2,1)} %bitcast.85), kind=kOutput, calls=%fused_computation.25 | convolution fusion | flops 1208033280 | bytes 11681792 | tf_op jit(solution)/shard_map/qhgsr,sgrd->qhd/dot_general | solution.py:87
  335.7 197.6 %reduce-scatter.2.cloned.1.call-done = f32[16,576]{1,0:T(8,128)} async-done(((f32[1024,576]{1,0:T(8,128)}), f32[16,576]{1,0:T(8,128)}) %reduce-scatter.2.cloned.1.call-update) | async-done | bytes 36880 | tf_op jit(solution)/shard_map/reduce_scatter | solution.py:82
  533.3 1.4 convert_element_type.21
  (31 shorter events, 0.5 us)
Async XLA Ops:
  7.2 182.6 %all-gather.6.cloned.1.call-start = ((), (), s32[]{:S(2)}) async-start(), calls=%async_computation.2 | async-start | bytes 10649600 | tf_op jit(solution)/shard_map/all_gather | solution.py:45
  8.9 220.9 %all-gather.8.cloned.1.call-start = ((), (), s32[]{:S(2)}) async-start(), calls=%async_computation.3 | async-start | bytes 1327104 | tf_op jit(solution)/shard_map/all_gather | solution.py:42
  9.7 268.9 %all-gather.10.cloned.1.call-start = ((), (), s32[]{:S(2)}) async-start(), calls=%async_computation.4 | async-start | bytes 1179648 | tf_op jit(solution)/shard_map/all_gather | solution.py:43
  10.4 522.8 %reduce-scatter.2.cloned.1.call-start = ((), (), s32[]{:S(2)}) async-start(), calls=%async_computation.5 | async-start | bytes 2662400 | tf_op jit(solution)/shard_map/reduce_scatter | solution.py:82
  233.0 21.7 %copy-start = (f32[1024,128,8]{1,0,2:T(8,128)}, f32[1024,128,8]{1,0,2:T(8,128)S(1)}, u32[]{:S(2)}) copy-start(f32[1024,128,8]{1,0,2:T(8,128)S(1)} %get-tuple-element.45) | copy-start | bytes 12582916
  299.1 5.0 copy-start.1
  299.1 5.1 copy-start.3
  304.2 1.3 copy-start.2
Sparse Core Ops, SparseCore 0:
  11.3 178.4 all-gather.5
  191.9 37.9 all-gather.7
  232.0 45.1 all-gather.9
  309.0 224.2 reduce-scatter.1
where the time goes:
time: 552 us; the launch traced here: 541 us
  waiting for transfers between devices  415 us (75%)
  blocking collectives  76.8 us (14%)
  matrix products  22.6 us (4%)
  between operations  13.9 us (3%)
  other arithmetic  9.27 us (2%)
    reduce_scatter x1, waiting for transfers between devices, local(): lax.psum_scatter(latent_part, 'seq', scatter_dimension=0, tiled=True)  198 us
    all_gather x1, waiting for transfers between devices, local(): all_keys = lax.all_gather(latent, 'seq', axis=0, tiled=True)  177 us
    all_gather x2, blocking collectives, merged(): pieces = jax.tree.map(lambda part: lax.all_gather(part, axis), value)  44.4 us
    all_gather x1, waiting for transfers between devices, local(): lax.all_gather(queries, 'head', axis=1, tiled=True)  38.6 us
    all_to_all x1, blocking collectives, local(): lax.all_to_all(score_grad, 'head', split_axis=1, concat_axis=2, tiled=True)  18.1 us
    psum x1, blocking collectives, local(): centred = lax.psum(jnp.sum(probabilities * prob_grad, axis=2), 'head')  14.3 us
  transfers between devices with their start and end apart: 4, of which 3 were waited for; matrix products, arithmetic and copies ran while one was open for 3% of the time, Pallas kernels for 0%

commit v1 on v0

v1 whole, which is shorter than its diff:
```python
import jax
import jax.numpy as jnp
from jax import lax
from jax.experimental import pallas as pl
from jax.experimental.pallas import tpu as pltpu
from jax.sharding import PartitionSpec as P

MESH = pl.DeviceIdType.MESH
F32, BF16 = jnp.float32, jnp.bfloat16
SCALE = 0.07216878364870322
FAR_BELOW = -1e30
NX, NZ = 4, 16
PIECE = 16
TILE = 256
NT = (((1,), (1,)), ((), ()))
NN = (((1,), (0,)), ((), ()))


def dot(a, b, dims=NN):
    return lax.dot_general(a, b, dims, preferred_element_type=F32)


def kernel(
    lat_ref, q_ref, do_ref, len_ref, dq_out, dk_out,
    krows, kbuf, ktr, kpos, qbuf, obuf, sc, dp, sg, pr,
    stat, comb, dk, ksend, krecv, rs_send, rs_recv, yh_send, yh_recv,
    dq_send, dq_recv, dq_own,
    gq_s, gq_r, go_s, go_r, kz_s, kz_r, kc_s, kc_r, st_s, st_r, dc_s, dc_r, rs_s, rs_r, dq_s, dq_r, misc_s, misc_r,
):
    seq, head = lax.axis_index("seq"), lax.axis_index("head")
    yh, z, c = seq // (2 * NZ), (seq // 2) % NZ, seq % 2
    x, yl = head // 2, head % 2

    def at(dx=0, dyl=0, dz=0, dc=0, dyh=0):
        seq_to = ((yh + dyh) % 2) * (2 * NZ) + ((z + dz + NZ) % NZ) * 2 + (c + dc) % 2
        return seq_to, ((x + dx) % NX) * 2 + (yl + dyl) % 2

    def send(src, dst, ssem, rsem, to):
        copy = pltpu.make_async_remote_copy(src, dst, ssem, rsem, device_id=to, device_id_type=MESH)
        copy.start()
        return copy

    me = at()
    pending = []

    peers = [at(dx=j // 2, dyl=j % 2) for j in range(1, 8)]
    peers += [at(dz=d) for d in (1, -1, 2, -2)]
    peers += [at(dc=1), at(dyh=1, dyl=1), at(dyh=1)]
    barrier = pltpu.get_barrier_semaphore()
    for peer in peers:
        pl.semaphore_signal(barrier, inc=1, device_id=peer, device_id_type=MESH)
    krows[...] = lat_ref[...].T
    pl.semaphore_wait(barrier, len(peers))

    def gather(n, src_slot, slot, to):
        if src_slot is None:
            q_src, o_src = q_ref, do_ref
        else:
            q_src, o_src = qbuf.at[src_slot], obuf.at[pl.ds(src_slot * 128, 128)]
        pending.append(send(q_src, qbuf.at[slot], gq_s.at[n], gq_r.at[slot], to))
        pending.append(send(o_src, obuf.at[pl.ds(slot * 128, 128)], go_s.at[n], go_r.at[slot], to))

    def arrived(slot):
        pltpu.make_async_remote_copy(q_ref, qbuf.at[slot], gq_s.at[0], gq_r.at[slot], device_id=me, device_id_type=MESH).wait_recv()
        pltpu.make_async_remote_copy(do_ref, obuf.at[pl.ds(slot * 128, 128)], go_s.at[0], go_r.at[slot], device_id=me, device_id_type=MESH).wait_recv()

    def chunk(o, core=0):
        return kbuf.at[pl.ds(core * 512 + (o % NZ) * 32, 32)]

    def krelay(o, delta):
        to = o - delta
        pending.append(send(chunk(o), chunk(to), kz_s.at[to % NZ], kz_r.at[to % NZ], at(dz=delta)))

    def kshare(o):
        pending.append(send(chunk(o), chunk(o, 1), kc_s.at[o % NZ], kc_r.at[o % NZ], at(dc=1)))

    def karrived(o):
        pltpu.make_async_remote_copy(chunk(o), chunk(o), kz_s.at[o % NZ], kz_r.at[o % NZ], device_id=me, device_id_type=MESH).wait_recv()

    adj = send(
        krows.at[pl.ds(pl.multiple_of((x * 2 + (1 - yl)) * PIECE, PIECE), PIECE)],
        kbuf.at[pl.ds(PIECE, PIECE)], misc_s.at[0], misc_r.at[0], at(dyh=1, dyl=1))
    gather(0, None, 1, at(dyl=1))
    gather(1, None, 6, at(dx=1))
    gather(2, None, 2, at(dx=-1 + NX))
    qbuf[0] = q_ref[...]
    obuf[pl.ds(0, 128)] = do_ref[...]
    kbuf[pl.ds(0, PIECE)] = krows[pl.ds(pl.multiple_of(head * PIECE, PIECE), PIECE)]

    adj.wait_recv()
    for delta in (-2, 2, -1, 1):
        krelay(0, delta)
    kshare(0)

    row = lax.broadcasted_iota(jnp.int32, kpos.shape, 0)
    r_c, r_z, r_y = row // 512, (row // 32) % NZ, (row // PIECE) % 2
    k_c, k_z, k_y = (c + r_c) % 2, (z + r_z) % NZ, (yh + r_y) % 2
    kpos[...] = (k_y * (2 * NZ) + k_z * 2 + k_c) * 128 + head * PIECE + row % PIECE
    qpos = seq * 128 + lax.broadcasted_iota(jnp.int32, (1, 128), 1)
    first = jnp.zeros((1, 128), jnp.int32)
    start = jnp.int32(0)
    for d in range(8):
        first = jnp.where(qpos >= start, start, first)
        start = start + len_ref[d]
    qpos2 = jnp.concatenate([qpos, qpos], axis=1)
    first2 = jnp.concatenate([first, first], axis=1)

    for o in (2, -2):
        karrived(o)
        krelay(o, -2 if o > 0 else 2)
        krelay(o, -1 if o > 0 else 1)
        kshare(o)
    arrived(1)
    gather(3, 1, 7, at(dx=1))
    gather(4, 1, 3, at(dx=-1 + NX))
    arrived(6)
    gather(5, 6, 4, at(dx=1))
    for o in (4, -4, 6, -6):
        karrived(o)
        if o != -6:
            krelay(o, -2 if o > 0 else 2)
        krelay(o, -1 if o > 0 else 1)
        kshare(o)
    for o in (1, -1, 3, -3, 5, -5, 7, -7, 8):
        karrived(o)
        kshare(o)
    arrived(3)
    gather(6, 3, 5, at(dx=-1 + NX))
    for o in range(NZ):
        pltpu.make_async_remote_copy(chunk(o), chunk(o, 1), kc_s.at[o], kc_r.at[o], device_id=me, device_id_type=MESH).wait_recv()

    def tile_rows(i):
        return pl.ds(pl.multiple_of(i * TILE, TILE), TILE)

    def absolute(slot):
        return ((x + slot // 2) % NX) * 2 + (yl + slot % 2) % 2

    def scores(t):
        qt = jnp.concatenate([qbuf[2 * t], qbuf[2 * t + 1]], axis=1)
        grads = obuf[pl.ds(t * TILE, TILE)]

        def first_pass(i, most):
            rows = tile_rows(i)
            keys = kbuf[rows]
            kp = jnp.concatenate([kpos[rows], kpos[rows]], axis=1)
            s = jnp.where((kp >= first2) & (kp <= qpos2), dot(keys, qt) * SCALE, FAR_BELOW)
            sc[t, rows] = s
            dp[t, rows] = dot(keys[:, :512], grads, NT)
            return jnp.maximum(most, jnp.max(s, axis=0, keepdims=True))

        most = lax.fori_loop(0, 4, first_pass, jnp.full((1, TILE), FAR_BELOW, F32))

        def second_pass(i, sums):
            rows = tile_rows(i)
            e = jnp.exp(sc[t, rows] - most)
            sc[t, rows] = e
            return sums[0] + jnp.sum(e, axis=0, keepdims=True), sums[1] + jnp.sum(e * dp[t, rows], axis=0, keepdims=True)

        zero = jnp.zeros((1, TILE), F32)
        total, weighted = lax.fori_loop(0, 4, second_pass, (zero, zero))
        for n, value in enumerate((most, total, weighted)):
            for half in range(2):
                stat[0, pl.ds(n * 8 + absolute(2 * t + half), 1), :] = value[:, half * 128:(half + 1) * 128]

    ktr[...] = kbuf[...].T
    scores(0)
    arrived(2)
    scores(1)
    arrived(7)
    scores(3)
    arrived(4)
    arrived(5)
    scores(2)

    for j in range(1, 8):
        back = ((-(j // 2)) % NX) * 2 + j % 2
        pending.append(send(stat.at[0], stat.at[back], st_s.at[j], st_r.at[back], at(dx=j // 2, dyl=j % 2)))
    for j in range(1, 8):
        pltpu.make_async_remote_copy(stat.at[0], stat.at[j], st_s.at[j], st_r.at[j], device_id=me, device_id_type=MESH).wait_recv()
    most = stat[0, 0:8]
    for j in range(1, 8):
        most = jnp.maximum(most, stat[j, 0:8])
    total, weighted = jnp.zeros((8, 128), F32), jnp.zeros((8, 128), F32)
    for j in range(8):
        factor = jnp.exp(stat[j, 0:8] - most)
        total += stat[j, 8:16] * factor
        weighted += stat[j, 16:24] * factor
    comb[0:8] = jnp.exp(stat[0, 0:8] - most) / total
    comb[8:16] = weighted / total

    for t in range(4):
        def row_of(n):
            return jnp.concatenate([comb[pl.ds(n * 8 + absolute(2 * t + half), 1), :] for half in range(2)], axis=1)

        gain, centre = row_of(0), row_of(1)

        def grads_of(i, carry):
            rows = tile_rows(i)
            p = sc[t, rows] * gain
            sg[rows, t * TILE:(t + 1) * TILE] = (p * (dp[t, rows] - centre) * SCALE).astype(BF16)
            pr[rows, t * TILE:(t + 1) * TILE] = p.astype(BF16)
            return carry

        lax.fori_loop(0, 4, grads_of, 0)

    def dk_tile(rows):
        whole = jnp.zeros((TILE, 576), F32)
        value = jnp.zeros((TILE, 512), F32)
        for t in range(4):
            cols = slice(t * TILE, (t + 1) * TILE)
            qt = jnp.concatenate([qbuf[2 * t], qbuf[2 * t + 1]], axis=1)
            whole += dot(sg[rows, cols], qt, NT)
            value += dot(pr[rows, cols], obuf[pl.ds(t * TILE, TILE)])
        return whole, value

    for half in range(2):
        whole, value = dk_tile(pl.ds(512 + half * TILE, TILE))
        rows = pl.ds(half * TILE, TILE)
        ksend[rows, :512] = (whole[:, :512] + value).astype(BF16)
        ksend[rows, 512:] = whole[:, 512:].astype(BF16)
        pending.append(send(ksend.at[rows], krecv.at[rows], dc_s.at[half], dc_r.at[half], at(dc=1)))
    for half in range(2):
        rows = pl.ds(half * TILE, TILE)
        whole, value = dk_tile(rows)
        dk[rows, :512] = whole[:, :512] + value
        dk[rows, 512:] = whole[:, 512:]
    for half in range(2):
        rows = pl.ds(half * TILE, TILE)
        pltpu.make_async_remote_copy(ksend.at[rows], krecv.at[rows], dc_s.at[half], dc_r.at[half], device_id=me, device_id_type=MESH).wait_recv()

    def rs_wait(o):
        i = o % NZ
        pltpu.make_async_remote_copy(rs_send.at[i], rs_recv.at[i], rs_s.at[i], rs_r.at[i], device_id=me, device_id_type=MESH).wait_recv()
        return rs_recv[i].astype(F32)

    def part(o, sources):
        rows = pl.ds((o % NZ) * 32, 32)
        acc = dk[rows] + krecv[rows].astype(F32)
        for source in sources:
            acc += rs_wait(source)
        return acc

    def rs_pass(o, delta, sources):
        i = o % NZ
        rs_send[i] = part(o, sources).astype(BF16)
        pending.append(send(rs_send.at[i], rs_recv.at[i], rs_s.at[i], rs_r.at[i], at(dz=delta)))

    def dq_pair(t):
        both = dot(ktr[...], sg[:, t * TILE:(t + 1) * TILE])
        for half in range(2):
            j = 2 * t + half
            value = both[:, half * 128:(half + 1) * 128]
            if j == 0:
                dq_own[...] = value
                continue
            dq_send[j] = value.astype(BF16)
            back = ((-(j // 2)) % NX) * 2 + j % 2
            pending.append(send(dq_send.at[j], dq_recv.at[back], dq_s.at[j], dq_r.at[back], at(dx=j // 2, dyl=j % 2)))

    rs_pass(8, 2, ())
    for o in (7, -7, 5, -5, 3, -3, 1, -1):
        rs_pass(o, 1 if o > 0 else -1, ())
    dq_pair(2)
    rs_pass(6, 2, (7, 8))
    rs_pass(-6, -2, (-7,))
    dq_pair(1)
    rs_pass(4, 2, (5, 6))
    rs_pass(-4, -2, (-5, -6))
    dq_pair(3)
    rs_pass(2, 2, (3, 4))
    rs_pass(-2, -2, (-3, -4))
    dq_pair(0)
    mine = part(0, (1, -1, 2, -2))
    yh_send[...] = mine[PIECE:].astype(BF16)
    last = send(yh_send, yh_recv, misc_s.at[1], misc_r.at[1], at(dyh=1))
    dq = dq_own[...]
    for j in range(1, 8):
        pltpu.make_async_remote_copy(dq_send.at[j], dq_recv.at[j], dq_s.at[j], dq_r.at[j], device_id=me, device_id_type=MESH).wait_recv()
        dq += dq_recv[j].astype(F32)
    dq_out[...] = dq.astype(BF16)
    last.wait_recv()
    dk_out[...] = (mine[:PIECE] + yh_recv[...].astype(F32)).astype(BF16)

    adj.wait_send()
    last.wait_send()
    for copy in pending:
        copy.wait_send()


def local(latent, queries, grad_out, doc_lengths):
    vmem = pl.BlockSpec(memory_space=pltpu.VMEM)
    sem = pltpu.SemaphoreType.DMA
    dq, dk = pl.pallas_call(
        kernel,
        out_shape=(jax.ShapeDtypeStruct((576, 128), BF16), jax.ShapeDtypeStruct((PIECE, 576), BF16)),
        in_specs=[vmem, vmem, vmem, pl.BlockSpec(memory_space=pltpu.SMEM)],
        out_specs=(vmem, vmem),
        scratch_shapes=[
            pltpu.VMEM((128, 576), BF16),
            pltpu.VMEM((1024, 576), BF16),
            pltpu.VMEM((576, 1024), BF16),
            pltpu.VMEM((1024, 128), jnp.int32),
            pltpu.VMEM((8, 576, 128), BF16),
            pltpu.VMEM((1024, 512), BF16),
            pltpu.VMEM((4, 1024, TILE), F32),
            pltpu.VMEM((4, 1024, TILE), F32),
            pltpu.VMEM((1024, 1024), BF16),
            pltpu.VMEM((1024, 1024), BF16),
            pltpu.VMEM((8, 24, 128), F32),
            pltpu.VMEM((16, 128), F32),
            pltpu.VMEM((512, 576), F32),
            pltpu.VMEM((512, 576), BF16),
            pltpu.VMEM((512, 576), BF16),
            pltpu.VMEM((NZ, 32, 576), BF16),
            pltpu.VMEM((NZ, 32, 576), BF16),
            pltpu.VMEM((PIECE, 576), BF16),
            pltpu.VMEM((PIECE, 576), BF16),
            pltpu.VMEM((8, 576, 128), BF16),
            pltpu.VMEM((8, 576, 128), BF16),
            pltpu.VMEM((576, 128), F32),
            sem((7,)), sem((8,)), sem((7,)), sem((8,)),
            sem((NZ,)), sem((NZ,)), sem((NZ,)), sem((NZ,)),
            sem((8,)), sem((8,)), sem((2,)), sem((2,)),
            sem((NZ,)), sem((NZ,)), sem((8,)), sem((8,)), sem((2,)), sem((2,)),
        ],
        compiler_params=pltpu.CompilerParams(collective_id=0, has_side_effects=True, vmem_limit_bytes=48 << 20),
        cost_estimate=pl.CostEstimate(flops=6_000_000_000, bytes_accessed=1_000_000, transcendentals=1_100_000),
        name="latent_attention_backward",
    )(latent.T, queries.reshape(128, 576).T, grad_out.reshape(128, 512), doc_lengths)
    return dq.T.reshape(128, 1, 576), dk


def solution(mesh):
    placed = (P("seq", None), P("seq", "head", None), P("seq", "head", None), P())
    return jax.shard_map(
        local,
        mesh=mesh,
        in_specs=placed,
        out_specs=(P("seq", "head", None), P(("seq", "head"), None)),
        check_vma=False,
    )
```

time: 552 us -> 82.1 us (0.15); the launches traced: 541 us -> 81.9 us
  waiting for transfers between devices: 415 us -> 0 us
  blocking collectives: 76.8 us -> 0 us
  Pallas kernels: 0 us -> 76.7 us
  matrix products: 22.6 us -> 0 us
  between operations: 13.9 us -> 0.65 us
  other arithmetic: 9.27 us -> 0 us
    all_gather x3 -> x0, waiting for transfers between devices: 216 us -> none  [the longest x1 177 us: local(): all_keys = lax.all_gather(latent, 'seq', axis=0, tiled=True)]
    reduce_scatter x1 -> x0, waiting for transfers between devices: 198 us -> none  [local(): lax.psum_scatter(latent_part, 'seq', scatter_dimension=0, tiled=True)]
    pallas_call x0 -> x1, Pallas kernels: none -> 76.7 us  [local(): pl.pallas_call(kernel, out_shape=(jax.ShapeDtypeStruct((576, 128), BF16),...]
    all_gather x2 -> x0, blocking collectives: 44.4 us -> none  [merged(): pieces = jax.tree.map(lambda part: lax.all_gather(part, axis), value)]
    dot_general x5 -> x0, matrix products: 22.6 us -> none  [the longest x1 8.68 us: local(): jnp.einsum('qhgsr,sgrd->qhd', arranged, grouped, preferred_element_type=j...]
    all_to_all x1 -> x0, blocking collectives: 18.1 us -> none  [local(): lax.all_to_all(score_grad, 'head', split_axis=1, concat_axis=2, tiled=True)]
    psum x1 -> x0, blocking collectives: 14.3 us -> none  [local(): centred = lax.psum(jnp.sum(probabilities * prob_grad, axis=2), 'head')]
    convert_element_type x2 -> x0, other arithmetic: 6.42 us -> none  [the longest x1 5.03 us: local(): (probabilities * (prob_grad - centred[..., None]) * softmax_scale).astype...]
  transfers between devices with their start and end apart: 4 -> 0, of which waited for: 3 -> 0; matrix products, arithmetic and copies ran while one was open for 3% -> 0% of each run, Pallas kernels for 0% -> 0%
where the time goes in v1:
time: 82.1 us; the launch traced here: 81.9 us
  Pallas kernels  76.7 us (93%)
  local copies, waits for them, and re-layouts  4.64 us (6%)
    pallas_call x1, Pallas kernels, local(): pl.pallas_call(kernel, out_shape=(jax.ShapeDtypeStruct((576, 128), BF16),...  76.7 us
    unnamed x10, local copies, waits for them, and re-layouts  4.64 us

profile of v1, /device:TPU:1, one launch (start us, length us, event | category | flops | bytes accessed | tf_op | source)
XLA Modules:
  0.0 81.9 jit_solution(5551765346001442033)
XLA Ops:
  0.6 0.0 copy-start.3
  0.6 0.6 copy-done.3
  1.3 0.0 copy-start
  1.3 0.9 %copy-done = bf16[128,576]{0,1:T(8,128)(2,1)S(1)} copy-done((bf16[128,576]{0,1:T(8,128)(2,1)S(1)}, bf16[128,576]{0,1:T(8,128)(2,1)}, u32[]{:S(2)}) %copy-start) | copy-done | bytes 147480
  2.2 0.0 copy-start.1
  2.2 0.9 %copy-done.1 = bf16[128,1,576]{0,2,1:T(8,128)(2,1)S(1)} copy-done((bf16[128,1,576]{0,2,1:T(8,128)(2,1)S(1)}, bf16[128,1,576]{0,2,1:T(8,128)(2,1)}, u32[]{:S(2)}) %copy-start.1) | copy-done | bytes 147480
  3.1 0.0 copy-start.2
  3.1 0.9 %copy-done.2 = bf16[128,1,512]{2,0,1:T(8,128)(2,1)S(1)} copy-done((bf16[128,1,512]{2,0,1:T(8,128)(2,1)S(1)}, bf16[128,1,512]{2,0,1:T(8,128)(2,1)}, u32[]{:S(2)}) %copy-start.2) | copy-done | bytes 131096
  4.0 76.7 %latent_attention_backward.1 = (bf16[576,128]{1,0:T(8,128)(2,1)S(1)}, bf16[16,576]{1,0:T(8,128)(2,1)S(1)}) custom-call(bf16[576,128]{1,0:T(8,128)(2,1)S(1)} %bitcast.9, bf16[576,128]{1,0:T(8,128)(2,1)S(1)} %bitcast.10, bf16[128,512]{1,0:T(8,128)(2,1)S(1)} %bitcast.11, s32[8]{0:T(128)S(1)} %copy-done.3), custom_call_target="tpu_custom_call" | custom-call | flops 6000000000 | bytes 1000000 | tf_op jit(solution)/shard_map/latent_attention_backward/pallas_call | solution.py:293
  80.7 0.7 copy.8
  81.3 0.6 copy.9
Async XLA Ops:
  0.6 0.7 copy-start.3
  1.3 0.9 %copy-start = (bf16[128,576]{0,1:T(8,128)(2,1)S(1)}, bf16[128,576]{0,1:T(8,128)(2,1)}, u32[]{:S(2)}) copy-start(bf16[128,576]{0,1:T(8,128)(2,1)} %param.4) | copy-start | bytes 442372
  2.2 0.9 %copy-start.1 = (bf16[128,1,576]{0,2,1:T(8,128)(2,1)S(1)}, bf16[128,1,576]{0,2,1:T(8,128)(2,1)}, u32[]{:S(2)}) copy-start(bf16[128,1,576]{0,2,1:T(8,128)(2,1)} %param.5) | copy-start | bytes 442372
  3.1 0.9 %copy-start.2 = (bf16[128,1,512]{2,0,1:T(8,128)(2,1)S(1)}, bf16[128,1,512]{2,0,1:T(8,128)(2,1)}, u32[]{:S(2)}) copy-start(bf16[128,1,512]{2,0,1:T(8,128)(2,1)} %param.6) | copy-start | bytes 393220

commit v2 on v1

v2 whole, which is shorter than its diff:
```python
import jax
import jax.numpy as jnp
from jax import lax
from jax.experimental import pallas as pl
from jax.experimental.pallas import tpu as pltpu
from jax.sharding import PartitionSpec as P

MESH = pl.DeviceIdType.MESH
F32, BF16 = jnp.float32, jnp.bfloat16
SCALE = 0.07216878364870322
FAR_BELOW = -1e30
NX, NZ = 4, 16
PIECE = 16
TILE = 256
NT = (((1,), (1,)), ((), ()))
NN = (((1,), (0,)), ((), ()))


def dot(a, b, dims=NN):
    return lax.dot_general(a, b, dims, preferred_element_type=F32)


def tree(step):
    above = {}
    for o in range(1, 9):
        above[o] = (o - 1) // step * step
    for o in range(1, 8):
        above[-o] = -((o - 1) // step * step)
    return above


GATHER, REDUCE = tree(3), tree(3)


def children(above, o):
    return sorted((k for k in above if above[k] == o), key=lambda k: (k not in above.values(), -abs(k), k))


def index(o):
    return (o + 3) % NZ


def kernel(
    lat_ref, q_ref, do_ref, len_ref, dq_out, dk_out,
    lat, krows, kbuf, ktr, kpos, qbuf, obuf, sc, dp, sg, pr,
    stat, comb, dk, ksend, krecv, rs_send, rs_recv, cross_recv,
    dq_send, dq_recv, dq_own,
    gq_s, gq_r, go_s, go_r, kz_s, kz_r, ka_s, ka_r, kc_s, kc_r, st_s, st_r, dc_s, dc_r, rs_s, rs_r, cr_s, cr_r, dq_s, dq_r, here_s,
):
    seq, head = lax.axis_index("seq"), lax.axis_index("head")
    yh, z, c = seq // (2 * NZ), (seq // 2) % NZ, seq % 2
    x, yl = head // 2, head % 2

    def at(dx=0, dyl=0, dz=0, dc=0, dyh=0):
        seq_to = ((yh + dyh) % 2) * (2 * NZ) + ((z + dz + NZ) % NZ) * 2 + (c + dc) % 2
        return seq_to, ((x + dx + NX) % NX) * 2 + (yl + dyl) % 2

    me = at()
    pending = []
    near = children(GATHER, 0)

    def remote(src, dst, ssem, rsem, to):
        return pltpu.make_async_remote_copy(src, dst, ssem, rsem, device_id=to, device_id_type=MESH)

    def send(*args):
        copy = remote(*args)
        copy.start()
        pending.append(copy)

    own = [
        pltpu.make_async_copy(lat_ref, lat, here_s.at[0]),
        pltpu.make_async_copy(q_ref, qbuf.at[0], here_s.at[1]),
        pltpu.make_async_copy(do_ref, obuf.at[pl.ds(0, 128)], here_s.at[2]),
    ]
    for copy in own:
        copy.start()
    peers = [at(dx=j // 2, dyl=j % 2) for j in range(1, 8)]
    peers += [at(dz=o) for o in near]
    peers += [at(dyh=1, dyl=1, dz=o) for o in [0] + near]
    peers += [at(dyh=1, dz=o) for o in [0] + near]
    peers += [at(dc=1)]
    barrier = pltpu.get_barrier_semaphore()
    for peer in peers:
        pl.semaphore_signal(barrier, inc=1, device_id=peer, device_id_type=MESH)
    own[0].wait()
    krows[...] = lat[...].T
    own[1].wait()
    own[2].wait()
    pl.semaphore_wait(barrier, len(peers))

    def grad_rows(slot):
        return obuf.at[pl.ds(slot * 128, 128)]

    def gather_q(n, src, slot, to):
        send(qbuf.at[src], qbuf.at[slot], gq_s.at[n], gq_r.at[slot], to)

    def gather_o(n, src, slot, to):
        send(grad_rows(src), grad_rows(slot), go_s.at[n], go_r.at[slot], to)

    def gather(n, src, slot, to):
        gather_q(n, src, slot, to)
        gather_o(n, src, slot, to)

    def arrived_q(slot):
        remote(qbuf.at[0], qbuf.at[slot], gq_s.at[0], gq_r.at[slot], me).wait_recv()

    def arrived_o(slot):
        remote(grad_rows(0), grad_rows(slot), go_s.at[0], go_r.at[slot], me).wait_recv()

    def chunk(o, core=0):
        return kbuf.at[pl.ds(core * 512 + index(o) * 32, 32)]

    def piece(o, plane):
        return kbuf.at[pl.ds(index(o) * 32 + plane * PIECE, PIECE)]

    own_piece = krows.at[pl.ds(pl.multiple_of(head * PIECE, PIECE), PIECE)]
    their_piece = krows.at[pl.ds(pl.multiple_of((x * 2 + (1 - yl)) * PIECE, PIECE), PIECE)]

    def first_spread(o):
        i = index(o)
        if o != 0:
            send(own_piece, piece(o, 0), kz_s.at[i], kz_r.at[i], at(dz=-o))
        send(their_piece, piece(o, 1), ka_s.at[i], ka_r.at[i], at(dyh=1, dyl=1, dz=-o))

    def share(o):
        i = index(o)
        send(chunk(o), chunk(o, 1), kc_s.at[i], kc_r.at[i], at(dc=1))

    def spread(o):
        for to in children(GATHER, o):
            n = index(to)
            send(chunk(o), chunk(to), kz_s.at[n], kz_r.at[n], at(dz=o - to))
        share(o)

    def karrived(o):
        i = index(o)
        if o in near:
            remote(own_piece, piece(o, 0), kz_s.at[i], kz_r.at[i], me).wait_recv()
        elif o != 0:
            remote(chunk(o), chunk(o), kz_s.at[i], kz_r.at[i], me).wait_recv()
        if o in near or o == 0:
            remote(their_piece, piece(o, 1), ka_s.at[i], ka_r.at[i], me).wait_recv()

    for o in near[:2]:
        first_spread(o)
    gather(0, 0, 6, at(dx=1))
    gather(1, 0, 2, at(dx=-1))
    gather(2, 0, 1, at(dyl=1))
    for o in [0] + near[2:]:
        first_spread(o)
    kbuf[pl.ds(index(0) * 32, PIECE)] = krows[pl.ds(pl.multiple_of(head * PIECE, PIECE), PIECE)]

    row = lax.broadcasted_iota(jnp.int32, kpos.shape, 0)
    r_c, r_z, r_y = row // 512, (row // 32) % NZ, (row // PIECE) % 2
    k_c, k_z, k_y = (c + r_c) % 2, (z + r_z + NZ - 3) % NZ, (yh + r_y) % 2
    kpos[...] = (k_y * (2 * NZ) + k_z * 2 + k_c) * 128 + head * PIECE + row % PIECE
    qpos = seq * 128 + lax.broadcasted_iota(jnp.int32, (1, 128), 1)
    first = jnp.zeros((1, 128), jnp.int32)
    start = jnp.int32(0)
    for d in range(8):
        first = jnp.where(qpos >= start, start, first)
        start = start + len_ref[d]
    qpos2 = jnp.concatenate([qpos, qpos], axis=1)
    first2 = jnp.concatenate([first, first], axis=1)
    waits = sorted(GATHER, key=lambda o: (abs(o), -o))
    hubs = [o for o in waits if children(GATHER, o)]
    for o in hubs[:2]:
        karrived(o)
        spread(o)
    arrived_q(6)
    gather_q(3, 6, 4, at(dx=1))
    arrived_o(2)
    gather_o(3, 2, 4, at(dx=-1))
    karrived(0)
    share(0)
    arrived_q(1)
    gather_q(4, 1, 7, at(dx=1))
    gather_q(5, 1, 3, at(dx=-1))
    arrived_o(1)
    gather_o(4, 1, 7, at(dx=1))
    gather_o(5, 1, 3, at(dx=-1))
    for o in hubs[2:]:
        karrived(o)
        spread(o)
    arrived_q(4)
    gather_q(6, 4, 5, at(dyl=1))
    arrived_o(4)
    gather_o(6, 4, 5, at(dyl=1))
    for o in waits:
        if o not in hubs:
            karrived(o)
            share(o)
    arrived_o(6)
    arrived_q(2)
    for o in range(NZ):
        i = index(o)
        remote(chunk(o), chunk(o, 1), kc_s.at[i], kc_r.at[i], me).wait_recv()

    def absolute(slot):
        return ((x + slot // 2) % NX) * 2 + (yl + slot % 2) % 2

    def queries_of(t):
        return jnp.concatenate([qbuf[2 * t], qbuf[2 * t + 1]], axis=1)

    def scores(t):
        qt = queries_of(t)
        grads = obuf[pl.ds(t * TILE, TILE)]
        most = jnp.full((1, TILE), FAR_BELOW, F32)
        for i in range(4):
            rows = pl.ds(i * TILE, TILE)
            keys = kbuf[rows]
            kp = jnp.concatenate([kpos[rows], kpos[rows]], axis=1)
            s = jnp.where((kp >= first2) & (kp <= qpos2), dot(keys, qt) * SCALE, FAR_BELOW)
            sc[t, rows] = s
            dp[t, rows] = dot(keys[:, :512], grads, NT)
            most = jnp.maximum(most, jnp.max(s, axis=0, keepdims=True))
        total = weighted = jnp.zeros((1, TILE), F32)
        for i in range(4):
            rows = pl.ds(i * TILE, TILE)
            e = jnp.exp(sc[t, rows] - most)
            sc[t, rows] = e
            total += jnp.sum(e, axis=0, keepdims=True)
            weighted += jnp.sum(e * dp[t, rows], axis=0, keepdims=True)
        for n, value in enumerate((most, total, weighted)):
            for half in range(2):
                stat[0, pl.ds(n * 8 + absolute(2 * t + half), 1), :] = value[:, half * 128:(half + 1) * 128]

    scores(0)
    for t in (1, 3, 2):
        for slot in {1: (3,), 3: (7,), 2: (5,)}[t]:
            arrived_q(slot)
            arrived_o(slot)
        scores(t)

    for j in (4, 5, 3, 7, 1, 2, 6):
        back = ((-(j // 2)) % NX) * 2 + j % 2
        send(stat.at[0], stat.at[back], st_s.at[j], st_r.at[back], at(dx=j // 2, dyl=j % 2))
    ktr[...] = kbuf[...].T
    for j in range(1, 8):
        remote(stat.at[0], stat.at[j], st_s.at[j], st_r.at[j], me).wait_recv()
    most = stat[0, 0:8]
    for j in range(1, 8):
        most = jnp.maximum(most, stat[j, 0:8])
    total, weighted = jnp.zeros((8, 128), F32), jnp.zeros((8, 128), F32)
    for j in range(8):
        factor = jnp.exp(stat[j, 0:8] - most)
        total += stat[j, 8:16] * factor
        weighted += stat[j, 16:24] * factor
    comb[0:8] = jnp.exp(stat[0, 0:8] - most) / total
    comb[8:16] = weighted / total

    def grads_of(i):
        rows = pl.ds(i * TILE, TILE)
        for t in range(4):
            gain, centre = (
                jnp.concatenate([comb[pl.ds(n * 8 + absolute(2 * t + half), 1), :] for half in range(2)], axis=1) for n in range(2))
            p = sc[t, rows] * gain
            sg[rows, t * TILE:(t + 1) * TILE] = (p * (dp[t, rows] - centre) * SCALE).astype(BF16)
            pr[rows, t * TILE:(t + 1) * TILE] = p.astype(BF16)

    def dk_tile(i, out, out_rows):
        rows = pl.ds(i * TILE, TILE)
        value = dot(pr[rows], obuf[...])
        whole = jnp.zeros((TILE, 576), F32)
        for t in range(4):
            whole += dot(sg[rows, t * TILE:(t + 1) * TILE], queries_of(t), NT)
        out[out_rows, :512] = (whole[:, :512] + value).astype(out.dtype)
        out[out_rows, 512:] = whole[:, 512:].astype(out.dtype)

    def dk_other(half):
        rows = pl.ds(half * TILE, TILE)
        dk_tile(2 + half, ksend, rows)
        send(ksend.at[rows], krecv.at[rows], dc_s.at[half], dc_r.at[half], at(dc=1))

    def dk_own(half):
        dk_tile(half, dk, pl.ds(half * TILE, TILE))

    def other_core(half):
        rows = pl.ds(half * TILE, TILE)
        remote(ksend.at[rows], krecv.at[rows], dc_s.at[half], dc_r.at[half], me).wait_recv()

    def part(o):
        rows = pl.ds(index(o) * 32, 32)
        acc = dk[rows] + krecv[rows].astype(F32)
        for source in children(REDUCE, o):
            i = index(source)
            remote(rs_send.at[i], rs_recv.at[i], rs_s.at[i], rs_r.at[i], me).wait_recv()
            acc += rs_recv[i].astype(F32)
        return acc

    def first_half(ref, o):
        return ref.at[index(o), pl.ds(0, PIECE)]

    def rs_pass(o):
        i = index(o)
        rs_send[i] = part(o).astype(BF16)
        if REDUCE[o] != 0:
            send(rs_send.at[i], rs_recv.at[i], rs_s.at[i], rs_r.at[i], at(dz=o - REDUCE[o]))
            return
        cross(o)
        send(first_half(rs_send, o), first_half(rs_recv, o), rs_s.at[i], rs_r.at[i], at(dz=o))

    def cross(o):
        i = index(o)
        send(rs_send.at[i, pl.ds(PIECE, PIECE)], cross_recv.at[i], cr_s.at[i], cr_r.at[i], at(dyh=1, dz=o))

    def dq_pair(t):
        both = dot(ktr[...], sg[:, t * TILE:(t + 1) * TILE])
        for half in range(2):
            j = 2 * t + half
            value = both[:, half * 128:(half + 1) * 128]
            if j == 0:
                dq_own[...] = value
                continue
            dq_send[j] = value.astype(BF16)
            back = ((-(j // 2)) % NX) * 2 + j % 2
            send(dq_send.at[j], dq_recv.at[back], dq_s.at[j], dq_r.at[back], at(dx=j // 2, dyl=j % 2))

    leaves = sorted((o for o in REDUCE if not children(REDUCE, o)), key=lambda o: (-abs(o), -o))
    inner = sorted((o for o in REDUCE if children(REDUCE, o)), key=lambda o: (-abs(o), -o))
    early = [o for o in leaves if index(o) >= 8]
    grads_of(3)
    dk_other(1)
    grads_of(1)
    dk_own(1)
    grads_of(2)
    grads_of(0)
    dq_pair(2)
    other_core(1)
    for o in early:
        rs_pass(o)
    dk_other(0)
    dk_own(0)
    dq_pair(1)
    other_core(0)
    for o in leaves:
        if o not in early:
            rs_pass(o)
    rs_send[index(0), PIECE:] = (dk[pl.ds(index(0) * 32 + PIECE, PIECE)] + krecv[pl.ds(index(0) * 32 + PIECE, PIECE)].astype(F32)).astype(BF16)
    cross(0)
    dq_pair(3)
    for o in inner[:2]:
        rs_pass(o)
    dq_pair(0)
    for o in inner[2:]:
        rs_pass(o)
    dq = dq_own[...]
    for j in (1, 2, 3, 6, 7, 4, 5):
        remote(dq_send.at[j], dq_recv.at[j], dq_s.at[j], dq_r.at[j], me).wait_recv()
        dq += dq_recv[j].astype(F32)
    dq_out[...] = dq.astype(BF16)
    rows = pl.ds(index(0) * 32, PIECE)
    total = dk[rows] + krecv[rows].astype(F32)
    for o in children(REDUCE, 0):
        i = index(o)
        remote(first_half(rs_send, o), first_half(rs_recv, o), rs_s.at[i], rs_r.at[i], me).wait_recv()
        total += rs_recv[i, :PIECE].astype(F32)
    for o in [0] + children(REDUCE, 0):
        i = index(o)
        remote(rs_send.at[i, pl.ds(PIECE, PIECE)], cross_recv.at[i], cr_s.at[i], cr_r.at[i], me).wait_recv()
        total += cross_recv[i].astype(F32)
    dk_out[...] = total.astype(BF16)
    for copy in pending:
        copy.wait_send()


def local(latent, queries, grad_out, doc_lengths):
    vmem = pl.BlockSpec(memory_space=pltpu.VMEM)
    hbm = pl.BlockSpec(memory_space=pltpu.HBM)
    sem = pltpu.SemaphoreType.DMA
    dq, dk = pl.pallas_call(
        kernel,
        out_shape=(jax.ShapeDtypeStruct((576, 128), BF16), jax.ShapeDtypeStruct((PIECE, 576), BF16)),
        in_specs=[hbm, hbm, hbm, pl.BlockSpec(memory_space=pltpu.SMEM)],
        out_specs=(vmem, vmem),
        scratch_shapes=[
            pltpu.VMEM((576, 128), BF16),
            pltpu.VMEM((128, 576), BF16),
            pltpu.VMEM((1024, 576), BF16),
            pltpu.VMEM((576, 1024), BF16),
            pltpu.VMEM((1024, 128), jnp.int32),
            pltpu.VMEM((8, 576, 128), BF16),
            pltpu.VMEM((1024, 512), BF16),
            pltpu.VMEM((4, 1024, TILE), F32),
            pltpu.VMEM((4, 1024, TILE), F32),
            pltpu.VMEM((1024, 1024), BF16),
            pltpu.VMEM((1024, 1024), BF16),
            pltpu.VMEM((8, 24, 128), F32),
            pltpu.VMEM((16, 128), F32),
            pltpu.VMEM((512, 576), F32),
            pltpu.VMEM((512, 576), BF16),
            pltpu.VMEM((512, 576), BF16),
            pltpu.VMEM((NZ, 32, 576), BF16),
            pltpu.VMEM((NZ, 32, 576), BF16),
            pltpu.VMEM((NZ, PIECE, 576), BF16),
            pltpu.VMEM((8, 576, 128), BF16),
            pltpu.VMEM((8, 576, 128), BF16),
            pltpu.VMEM((576, 128), F32),
            sem((7,)), sem((8,)), sem((7,)), sem((8,)),
            sem((NZ,)), sem((NZ,)), sem((NZ,)), sem((NZ,)), sem((NZ,)), sem((NZ,)),
            sem((8,)), sem((8,)), sem((2,)), sem((2,)),
            sem((NZ,)), sem((NZ,)), sem((NZ,)), sem((NZ,)), sem((8,)), sem((8,)), sem((3,)),
        ],
        compiler_params=pltpu.CompilerParams(collective_id=0, has_side_effects=True, vmem_limit_bytes=60 << 20),
        cost_estimate=pl.CostEstimate(flops=6_000_000_000, bytes_accessed=1_000_000, transcendentals=1_100_000),
        name="latent_attention_backward",
    )(latent.T, queries.reshape(128, 576).T, grad_out.reshape(128, 512), doc_lengths)
    return dq.T.reshape(128, 1, 576), dk


def solution(mesh):
    placed = (P("seq", None), P("seq", "head", None), P("seq", "head", None), P())
    return jax.shard_map(
        local,
        mesh=mesh,
        in_specs=placed,
        out_specs=(P("seq", "head", None), P(("seq", "head"), None)),
        check_vma=False,
    )
```

time: 82.1 us -> 71.7 us (0.87)
  Pallas kernels: 76.7 us -> 68.7 us
  local copies, waits for them, and re-layouts: 4.64 us -> 2.2 us
    pallas_call x1, Pallas kernels: 76.7 us -> 68.7 us  [local(): pl.pallas_call(kernel, out_shape=(jax.ShapeDtypeStruct((576, 128), BF16),...]
    unnamed x10 -> x4, local copies, waits for them, and re-layouts: 4.64 us -> 2.2 us
where the time goes in v2:
time: 71.7 us; the launch traced here: 71.6 us
  Pallas kernels  68.7 us (96%)
  local copies, waits for them, and re-layouts  2.2 us (3%)
    pallas_call x1, Pallas kernels, local(): pl.pallas_call(kernel, out_shape=(jax.ShapeDtypeStruct((576, 128), BF16),...  68.7 us
    unnamed x4, local copies, waits for them, and re-layouts  2.2 us

profile of v2, /device:TPU:1, one launch (start us, length us, event | category | flops | bytes accessed | tf_op | source)
XLA Modules:
  0.0 71.6 jit_solution(4102304268004727674)
XLA Ops:
  0.6 68.7 %latent_attention_backward.1 = (bf16[576,128]{1,0:T(8,128)(2,1)}, bf16[16,576]{1,0:T(8,128)(2,1)}) custom-call(bf16[576,128]{1,0:T(8,128)(2,1)} %bitcast.9, bf16[576,128]{1,0:T(8,128)(2,1)} %bitcast.10, bf16[128,512]{1,0:T(8,128)(2,1)} %bitcast.11, s32[8]{0:T(128)} %len_ref.1), custom_call_target="tpu_custom_call" | custom-call | flops 6000000000 | bytes 1000000 | tf_op jit(solution)/shard_map/latent_attention_backward/pallas_call | solution.py:371
  69.4 0.0 copy-start
  69.4 1.6 %copy.8 = bf16[128,1,576]{0,2,1:T(8,128)(2,1)} copy(bf16[128,1,576]{0,2,1:T(8,128)(2,1)} %bitcast.8) | data formatting | bytes 294912
  71.0 0.0 copy-done
  71.0 0.6 copy.9
Async XLA Ops:
  69.4 1.6 %copy-start = (bf16[16,576]{1,0:T(8,128)(2,1)S(1)}, bf16[16,576]{1,0:T(8,128)(2,1)}, u32[]{:S(2)}) copy-start(bf16[16,576]{1,0:T(8,128)(2,1)} %get-tuple-element.9) | copy-start | bytes 55300

commit v3 on v2

--- a/solution.py
+++ b/solution.py
@@ -29,7 +29,7 @@
     return above
 
 
-GATHER, REDUCE = tree(3), tree(3)
+GATHER, REDUCE = tree(3), tree(2)
 
 
 def children(above, o):
@@ -186,15 +186,7 @@
     gather_q(6, 4, 5, at(dyl=1))
     arrived_o(4)
     gather_o(6, 4, 5, at(dyl=1))
-    for o in waits:
-        if o not in hubs:
-            karrived(o)
-            share(o)
-    arrived_o(6)
-    arrived_q(2)
-    for o in range(NZ):
-        i = index(o)
-        remote(chunk(o), chunk(o, 1), kc_s.at[i], kc_r.at[i], me).wait_recv()
+    most, total, weighted = {}, {}, {}
 
     def absolute(slot):
         return ((x + slot // 2) % NX) * 2 + (yl + slot % 2) % 2
@@ -202,35 +194,62 @@
     def queries_of(t):
         return jnp.concatenate([qbuf[2 * t], qbuf[2 * t + 1]], axis=1)
 
-    def scores(t):
+    def scores(t, tiles):
         qt = queries_of(t)
         grads = obuf[pl.ds(t * TILE, TILE)]
-        most = jnp.full((1, TILE), FAR_BELOW, F32)
-        for i in range(4):
+        for i in tiles:
             rows = pl.ds(i * TILE, TILE)
             keys = kbuf[rows]
             kp = jnp.concatenate([kpos[rows], kpos[rows]], axis=1)
             s = jnp.where((kp >= first2) & (kp <= qpos2), dot(keys, qt) * SCALE, FAR_BELOW)
             sc[t, rows] = s
             dp[t, rows] = dot(keys[:, :512], grads, NT)
-            most = jnp.maximum(most, jnp.max(s, axis=0, keepdims=True))
-        total = weighted = jnp.zeros((1, TILE), F32)
+            top = jnp.max(s, axis=0, keepdims=True)
+            most[t] = jnp.maximum(most[t], top) if t in most else top
+
+    def weights(t):
+        total[t] = weighted[t] = jnp.zeros((1, TILE), F32)
         for i in range(4):
             rows = pl.ds(i * TILE, TILE)
-            e = jnp.exp(sc[t, rows] - most)
+            e = jnp.exp(sc[t, rows] - most[t])
             sc[t, rows] = e
-            total += jnp.sum(e, axis=0, keepdims=True)
-            weighted += jnp.sum(e * dp[t, rows], axis=0, keepdims=True)
-        for n, value in enumerate((most, total, weighted)):
+            total[t] += jnp.sum(e, axis=0, keepdims=True)
+            weighted[t] += jnp.sum(e * dp[t, rows], axis=0, keepdims=True)
+        for n, value in enumerate((most[t], total[t], weighted[t])):
             for half in range(2):
                 stat[0, pl.ds(n * 8 + absolute(2 * t + half), 1), :] = value[:, half * 128:(half + 1) * 128]
 
-    scores(0)
-    for t in (1, 3, 2):
-        for slot in {1: (3,), 3: (7,), 2: (5,)}[t]:
-            arrived_q(slot)
-            arrived_o(slot)
-        scores(t)
+    def keys_in(offsets):
+        for o in offsets:
+            if o not in hubs:
+                karrived(o)
+                share(o)
+
+    def other_keys_in(offsets):
+        for o in offsets:
+            i = index(o)
+            remote(chunk(o), chunk(o, 1), kc_s.at[i], kc_r.at[i], me).wait_recv()
+
+    close = [o for o in waits if index(o) < 8]
+    distant = [o for o in waits if index(o) >= 8]
+    keys_in(close)
+    other_keys_in([0] + close)
+    scores(0, (0, 2))
+    keys_in(distant)
+    arrived_o(6)
+    arrived_q(2)
+    for t, slot in ((1, 3), (3, 7)):
+        arrived_q(slot)
+        arrived_o(slot)
+        scores(t, (0, 2))
+    other_keys_in(distant)
+    for t in (0, 1, 3):
+        scores(t, (1, 3))
+        weights(t)
+    arrived_q(5)
+    arrived_o(5)
+    scores(2, range(4))
+    weights(2)
 
     for j in (4, 5, 3, 7, 1, 2, 6):
         back = ((-(j // 2)) % NX) * 2 + j % 2
@@ -238,16 +257,16 @@
     ktr[...] = kbuf[...].T
     for j in range(1, 8):
         remote(stat.at[0], stat.at[j], st_s.at[j], st_r.at[j], me).wait_recv()
-    most = stat[0, 0:8]
+    top = stat[0, 0:8]
     for j in range(1, 8):
-        most = jnp.maximum(most, stat[j, 0:8])
-    total, weighted = jnp.zeros((8, 128), F32), jnp.zeros((8, 128), F32)
+        top = jnp.maximum(top, stat[j, 0:8])
+    whole_total, whole_weighted = jnp.zeros((8, 128), F32), jnp.zeros((8, 128), F32)
     for j in range(8):
-        factor = jnp.exp(stat[j, 0:8] - most)
-        total += stat[j, 8:16] * factor
-        weighted += stat[j, 16:24] * factor
-    comb[0:8] = jnp.exp(stat[0, 0:8] - most) / total
-    comb[8:16] = weighted / total
+        factor = jnp.exp(stat[j, 0:8] - top)
+        whole_total += stat[j, 8:16] * factor
+        whole_weighted += stat[j, 16:24] * factor
+    comb[0:8] = jnp.exp(stat[0, 0:8] - top) / whole_total
+    comb[8:16] = whole_weighted / whole_total
 
     def grads_of(i):
         rows = pl.ds(i * TILE, TILE)
@@ -319,26 +338,25 @@
     leaves = sorted((o for o in REDUCE if not children(REDUCE, o)), key=lambda o: (-abs(o), -o))
     inner = sorted((o for o in REDUCE if children(REDUCE, o)), key=lambda o: (-abs(o), -o))
     early = [o for o in leaves if index(o) >= 8]
-    grads_of(3)
+    for i in (3, 1, 2, 0):
+        grads_of(i)
+    dq_pair(2)
     dk_other(1)
-    grads_of(1)
     dk_own(1)
-    grads_of(2)
-    grads_of(0)
-    dq_pair(2)
+    dq_pair(1)
     other_core(1)
     for o in early:
         rs_pass(o)
+    dq_pair(3)
     dk_other(0)
     dk_own(0)
-    dq_pair(1)
     other_core(0)
     for o in leaves:
         if o not in early:
             rs_pass(o)
-    rs_send[index(0), PIECE:] = (dk[pl.ds(index(0) * 32 + PIECE, PIECE)] + krecv[pl.ds(index(0) * 32 + PIECE, PIECE)].astype(F32)).astype(BF16)
+    rows = pl.ds(index(0) * 32 + PIECE, PIECE)
+    rs_send[index(0), PIECE:] = (dk[rows] + krecv[rows].astype(F32)).astype(BF16)
     cross(0)
-    dq_pair(3)
     for o in inner[:2]:
         rs_pass(o)
     dq_pair(0)
@@ -368,6 +386,7 @@
     vmem = pl.BlockSpec(memory_space=pltpu.VMEM)
     hbm = pl.BlockSpec(memory_space=pltpu.HBM)
     sem = pltpu.SemaphoreType.DMA
+    arrays = latent.T, queries.reshape(128, 576).T, grad_out.reshape(128, 512), doc_lengths
     dq, dk = pl.pallas_call(
         kernel,
         out_shape=(jax.ShapeDtypeStruct((576, 128), BF16), jax.ShapeDtypeStruct((PIECE, 576), BF16)),
@@ -401,10 +420,10 @@
             sem((8,)), sem((8,)), sem((2,)), sem((2,)),
             sem((NZ,)), sem((NZ,)), sem((NZ,)), sem((NZ,)), sem((8,)), sem((8,)), sem((3,)),
         ],
-        compiler_params=pltpu.CompilerParams(collective_id=0, has_side_effects=True, vmem_limit_bytes=60 << 20),
+        compiler_params=pltpu.CompilerParams(collective_id=0, has_side_effects=True, vmem_limit_bytes=48 << 20),
         cost_estimate=pl.CostEstimate(flops=6_000_000_000, bytes_accessed=1_000_000, transcendentals=1_100_000),
         name="latent_attention_backward",
-    )(latent.T, queries.reshape(128, 576).T, grad_out.reshape(128, 512), doc_lengths)
+    )(*(pltpu.with_memory_space_constraint(array, pltpu.HBM) for array in arrays))
     return dq.T.reshape(128, 1, 576), dk
 
 

time: 71.7 us -> 67.7 us (0.944)
  Pallas kernels: 68.7 us -> 65.5 us
  local copies, waits for them, and re-layouts: 2.2 us -> 1.27 us
    pallas_call x1, Pallas kernels: 68.7 us -> 65.5 us  [local(): pl.pallas_call(kernel, out_shape=(jax.ShapeDtypeStruct((576, 128), BF16),...]
    unnamed x4 -> x2, local copies, waits for them, and re-layouts: 2.2 us -> 1.27 us
where the time goes in v3:
time: 67.7 us; the launch traced here: 67.4 us
  Pallas kernels  65.5 us (97%)
  local copies, waits for them, and re-layouts  1.27 us (2%)
    pallas_call x1, Pallas kernels, local(): pl.pallas_call(kernel, out_shape=(jax.ShapeDtypeStruct((576, 128), BF16),...  65.5 us

profile of v3, /device:TPU:1, one launch (start us, length us, event | category | flops | bytes accessed | tf_op | source)
XLA Modules:
  0.0 67.4 jit_solution(16233146233526583170)
XLA Ops:
  0.6 65.5 %latent_attention_backward.1 = (bf16[576,128]{1,0:T(8,128)(2,1)S(1)}, bf16[16,576]{1,0:T(8,128)(2,1)S(1)}) custom-call(bf16[576,128]{1,0:T(8,128)(2,1)} %bitcast.9, bf16[576,128]{1,0:T(8,128)(2,1)} %bitcast.10, bf16[128,512]{1,0:T(8,128)(2,1)} %bitcast.11, s32[8]{0:T(128)} %len_ref.1), custom_call_target="tpu_custom_call" | custom-call | flops 6000000000 | bytes 1000000 | tf_op jit(solution)/shard_map/latent_attention_backward/pallas_call | solution.py:390
  66.1 0.7 copy.8
  66.8 0.6 copy.9

commit v4 on v3

--- a/solution.py
+++ b/solution.py
@@ -66,6 +66,11 @@
         copy = remote(*args)
         copy.start()
         pending.append(copy)
+
+    def sent(count):
+        for copy in pending[:count]:
+            copy.wait_send()
+        del pending[:count]
 
     own = [
         pltpu.make_async_copy(lat_ref, lat, here_s.at[0]),
@@ -254,6 +259,7 @@
     for j in (4, 5, 3, 7, 1, 2, 6):
         back = ((-(j // 2)) % NX) * 2 + j % 2
         send(stat.at[0], stat.at[back], st_s.at[j], st_r.at[back], at(dx=j // 2, dyl=j % 2))
+    sent(len(pending) - 7)
     ktr[...] = kbuf[...].T
     for j in range(1, 8):
         remote(stat.at[0], stat.at[j], st_s.at[j], st_r.at[j], me).wait_recv()
@@ -362,6 +368,7 @@
     dq_pair(0)
     for o in inner[2:]:
         rs_pass(o)
+    sent(7 + 2)
     dq = dq_own[...]
     for j in (1, 2, 3, 6, 7, 4, 5):
         remote(dq_send.at[j], dq_recv.at[j], dq_s.at[j], dq_r.at[j], me).wait_recv()
@@ -378,8 +385,7 @@
         remote(rs_send.at[i, pl.ds(PIECE, PIECE)], cross_recv.at[i], cr_s.at[i], cr_r.at[i], me).wait_recv()
         total += cross_recv[i].astype(F32)
     dk_out[...] = total.astype(BF16)
-    for copy in pending:
-        copy.wait_send()
+    sent(len(pending))
 
 
 def local(latent, queries, grad_out, doc_lengths):

time: 67.7 us -> 67.6 us (level)
  no operation moved by 1% of the time
where the time goes in v4:
time: 67.6 us; the launch traced here: 67.3 us
  Pallas kernels  65.4 us (97%)
  local copies, waits for them, and re-layouts  1.27 us (2%)
    pallas_call x1, Pallas kernels, local(): pl.pallas_call(kernel, out_shape=(jax.ShapeDtypeStruct((576, 128), BF16),...  65.4 us

profile of v4, /device:TPU:1, one launch (start us, length us, event | category | flops | bytes accessed | tf_op | source)
XLA Modules:
  0.0 67.3 jit_solution(13919132579107491921)
XLA Ops:
  0.6 65.4 %latent_attention_backward.1 = (bf16[576,128]{1,0:T(8,128)(2,1)S(1)}, bf16[16,576]{1,0:T(8,128)(2,1)S(1)}) custom-call(bf16[576,128]{1,0:T(8,128)(2,1)} %bitcast.9, bf16[576,128]{1,0:T(8,128)(2,1)} %bitcast.10, bf16[128,512]{1,0:T(8,128)(2,1)} %bitcast.11, s32[8]{0:T(128)} %len_ref.1), custom_call_target="tpu_custom_call" | custom-call | flops 6000000000 | bytes 1000000 | tf_op jit(solution)/shard_map/latent_attention_backward/pallas_call | solution.py:396
  66.0 0.7 copy.8
  66.7 0.6 copy.9
